TPU v7x, 32 devices: a whole 2x2x4 slice. The times are simulated.
32 devices in a mesh: parts: 2 (over y), seq: 4 (over z), tensor: 4 (over x, core).
Axes of the slice: x: 2, y: 2, z: 4, core: 2. Of those that a mesh axis runs over, the one named last changes fastest.
Arguments:
- query: bfloat16 [2048, 8192], P(('parts', 'seq'), 'tensor'), parts along dimension 0, may hold values from -6 to 6
- keys: bfloat16 [384, 1024], P(('parts', 'seq'), 'tensor'), parts along dimension 0, may hold values from -6 to 6
- values: bfloat16 [384, 1024], P(('parts', 'seq'), 'tensor'), parts along dimension 0, may hold values from -6 to 6
- q_gain: float32 [128], replicated, may hold values from 0.1 to 1.9
- key_norm_gain: float32 [128], replicated, may hold values from 0.1 to 1.9
- gate: float32 [64], P('tensor'), may hold values from 0.2 to 3
- grad_out: bfloat16 [2048, 8192], P(('parts', 'seq'), 'tensor'), parts along dimension 0, may hold values from -144 to 144
Outputs:
- query_grad: bfloat16 [2048, 8192], P(('parts', 'seq'), 'tensor'), parts along dimension 0
- projected_key_gradient: bfloat16 [384, 1024], P(('parts', 'seq'), 'tensor'), parts along dimension 0
- projected_value_gradient: bfloat16 [384, 1024], P(('parts', 'seq'), 'tensor'), parts along dimension 0
There are 2 independent parts, one for each index of `parts`. A program takes and returns all parts, laid end to end along the dimension named above; an argument that names none is the same for every part. Nothing has to cross between parts.
All inputs are finite; a program needn't handle non-finite values.
Results may differ from a plain program's by a relative error of at most 0.0087.
Values may be sent and summed in bfloat16 or wider, within the bound.
A program may use at most 64 MiB of HBM per device.

v0:
```python
import math

import jax
import jax.numpy as jnp
from jax import lax
from jax.sharding import PartitionSpec as P

HEAD_SIZE = 128


eps_value = 1e-05
block_rows = 512


def rms_norm_forward(raw, gain, head_count):
    count_rows = raw.shape[0]
    wide = raw.astype(jnp.float32).reshape(count_rows, head_count, raw.shape[1] // head_count)
    recip = lax.rsqrt(jnp.mean(wide * wide, axis=-1, keepdims=True) + eps_value)
    return (wide, recip, (wide * recip * gain).astype(jnp.bfloat16))


def rms_norm_backward(wide, recip, gain, upstream):
    scaled = gain * upstream
    return recip * scaled - wide * (recip * recip * recip) * jnp.mean(
        wide * scaled, axis=-1, keepdims=True
    )


def to_groups(wide, kv_heads):
    count_rows, head_count, head_width = wide.shape
    head_group = head_count // kv_heads
    return (
        wide.reshape(count_rows, kv_heads, head_group, head_width)
        .transpose(1, 2, 0, 3)
        .reshape(kv_heads, head_group * count_rows, head_width)
    )


def from_groups(grouped, count_rows):
    kv_heads, stacked, head_width = grouped.shape
    head_group = stacked // count_rows
    return (
        grouped.reshape(kv_heads, head_group, count_rows, head_width)
        .transpose(2, 0, 1, 3)
        .reshape(count_rows, kv_heads * head_group, head_width)
    )


def run_blocks(step_fn, running, key_rows, value_rows):
    total_rows = key_rows.shape[0]
    block_size = min(total_rows, block_rows)
    full_blocks = total_rows // block_size
    key_blocks = key_rows.reshape(full_blocks, block_size, key_rows.shape[1])
    value_blocks = value_rows.reshape(full_blocks, block_size, value_rows.shape[1])

    def advance(state, sliced):
        key_block, value_block, block_index = sliced
        return (step_fn(state, key_block, value_block, block_index * block_size), None)

    running, _ = lax.scan(
        advance, running, (key_blocks, value_blocks, jnp.arange(full_blocks, dtype=jnp.int32))
    )
    return running


def shards(query, keys, values, q_gain, key_norm_gain, gate, grad_out):
    text_rows = query.shape[0]
    q_heads = query.shape[1] // HEAD_SIZE
    kv_heads = keys.shape[1] // HEAD_SIZE
    audio_frame_rows = keys.shape[0]
    kv_width = kv_heads * HEAD_SIZE
    score_scale = 1.0 / math.sqrt(HEAD_SIZE)
    q_wide, q_recip, q_normed = rms_norm_forward(query, q_gain, q_heads)
    key_widened, key_reciprocal, key_normalized = rms_norm_forward(keys, key_norm_gain, kv_heads)
    k_flat = key_normalized.reshape(audio_frame_rows, kv_width)
    q_groups = to_groups(q_normed, kv_heads)
    go_wide = (
        grad_out.astype(jnp.float32).reshape(text_rows, q_heads, HEAD_SIZE)
        * jnp.tanh(gate)[None, :, None]
    )
    go_groups_full = to_groups(go_wide, kv_heads)
    go_groups = go_groups_full.astype(jnp.bfloat16)
    stacked = q_groups.shape[1]
    frames_all = audio_frame_rows * lax.axis_size("seq")

    def scores_of(key_piece):
        key_heads = key_piece.reshape(key_piece.shape[0], kv_heads, HEAD_SIZE)
        logits = (
            jnp.einsum("cmd,ncd->cmn", q_groups, key_heads, preferred_element_type=jnp.float32)
            * score_scale
        )
        return (key_heads, logits)

    def forward_step(running, key_piece, value_piece, offset):
        row_sums, out_accum = running
        key_heads, logits = scores_of(key_piece)
        exp_scores = jnp.exp(logits)
        heads_of_value = value_piece.reshape(value_piece.shape[0], kv_heads, HEAD_SIZE)
        out_accum = out_accum + jnp.einsum(
            "cmn,ncd->cmd",
            exp_scores.astype(jnp.bfloat16),
            heads_of_value,
            preferred_element_type=jnp.float32,
        )
        return (row_sums + jnp.sum(exp_scores, axis=-1), out_accum)

    def backward_terms(key_piece, value_piece, row_sums, row_delta):
        piece_rows = key_piece.shape[0]
        key_heads, logits = scores_of(key_piece)
        weights = jnp.exp(logits) / row_sums[..., None]
        heads_of_value = value_piece.reshape(piece_rows, kv_heads, HEAD_SIZE)
        grad_probs = jnp.einsum(
            "cmd,ncd->cmn", go_groups, heads_of_value, preferred_element_type=jnp.float32
        )
        grad_scores = (weights * (grad_probs - row_delta[..., None])).astype(jnp.bfloat16)
        value_part = jnp.einsum(
            "cmn,cmd->ncd",
            weights.astype(jnp.bfloat16),
            go_groups,
            preferred_element_type=jnp.float32,
        )
        key_part = (
            jnp.einsum("cmn,cmd->ncd", grad_scores, q_groups, preferred_element_type=jnp.float32)
            * score_scale
        )
        query_part = (
            jnp.einsum("cmn,ncd->cmd", grad_scores, key_heads, preferred_element_type=jnp.float32)
            * score_scale
        )
        kv_part = jnp.concatenate(
            [key_part.reshape(piece_rows, kv_width), value_part.reshape(piece_rows, kv_width)],
            axis=1,
        )
        return (query_part, kv_part)

    forward_init = (
        jnp.zeros((kv_heads, stacked), jnp.float32),
        jnp.zeros((kv_heads, stacked, HEAD_SIZE), jnp.float32),
    )
    query_zero = jnp.zeros((kv_heads, stacked, HEAD_SIZE), jnp.float32)
    buffer_zero = jnp.zeros((frames_all, 2 * kv_width), jnp.float32)
    pieces = (
        lax.all_gather(k_flat, "seq", axis=0, tiled=True),
        lax.all_gather(values, "seq", axis=0, tiled=True),
    )
    row_sums, out_accum = run_blocks(forward_step, forward_init, pieces[0], pieces[1])
    output = out_accum / row_sums[..., None]
    row_delta = jnp.sum(go_groups_full * output, axis=-1)

    def backward_step(running, key_piece, value_piece, offset):
        query_acc, buffer = running
        query_part, kv_part = backward_terms(key_piece, value_piece, row_sums, row_delta)
        return (query_acc + query_part, lax.dynamic_update_slice_in_dim(buffer, kv_part, offset, 0))

    pieces = (
        lax.all_gather(k_flat, "seq", axis=0, tiled=True),
        lax.all_gather(values, "seq", axis=0, tiled=True),
    )
    query_acc, buffer = run_blocks(backward_step, (query_zero, buffer_zero), pieces[0], pieces[1])
    kv_grads = lax.psum_scatter(buffer, "seq", scatter_dimension=0, tiled=True)
    query_wide = from_groups(query_acc, text_rows)
    query_grad = (
        rms_norm_backward(q_wide, q_recip, q_gain, query_wide)
        .reshape(text_rows, q_heads * HEAD_SIZE)
        .astype(jnp.bfloat16)
    )
    key_gradient_sum = kv_grads[:, :kv_width].reshape(audio_frame_rows, kv_heads, HEAD_SIZE)
    projected_key_gradient = (
        rms_norm_backward(key_widened, key_reciprocal, key_norm_gain, key_gradient_sum)
        .reshape(audio_frame_rows, kv_width)
        .astype(jnp.bfloat16)
    )
    projected_value_gradient = kv_grads[:, kv_width:].astype(jnp.bfloat16)
    return (query_grad, projected_key_gradient, projected_value_gradient)


def solution(mesh):
    placed = (
        P(("parts", "seq"), "tensor"),
        P(("parts", "seq"), "tensor"),
        P(("parts", "seq"), "tensor"),
        P(),
        P(),
        P("tensor"),
        P(("parts", "seq"), "tensor"),
    )
    return jax.shard_map(
        shards,
        mesh=mesh,
        in_specs=placed,
        out_specs=(
            P(("parts", "seq"), "tensor"),
            P(("parts", "seq"), "tensor"),
            P(("parts", "seq"), "tensor"),
        ),
        check_vma=False,
    )
```

profile of v0, /device:TPU:0, one launch (start us, length us, event | category | flops | bytes accessed | tf_op | source)
XLA Modules:
  0.0 90.2 jit_solution(11712292627705008678)
XLA Ops:
  7.2 1.5 %convert_bitcast_fusion = f32[32,8,16,128]{3,1,2,0:T(8,128)S(1)} fusion(bf16[256,2048]{1,0:T(8,128)(2,1)} %param.7), kind=kLoop, calls=%fused_computation.4 | loop fusion | flops 524288 | bytes 3145728
  9.1 0.6 multiply_reduce_fusion
  10.0 0.7 fusion.17
  11.3 15.0 %all_gather.8 = bf16[192,256]{1,0:T(8,128)(2,1)S(1)} all-gather(bf16[48,256]{1,0:T(8,128)(2,1)S(1)} %fusion.31), channel_id=1, replica_groups=mesh['parts'=2,'seq'=4,'tensor'=4] {'seq'}, dimensions={0}, use_global_device_ids=true | all-gather | bytes 122880 | tf_op jit(solution)/shard_map/all_gather | solution.py:156
  26.4 1.5 %convert_bitcast_fusion.1 = f32[32,8,16,128]{3,1,2,0:T(8,128)S(1)} fusion(bf16[256,2048]{1,0:T(8,128)(2,1)} %param.13), kind=kLoop, calls=%fused_computation.15 | loop fusion | flops 524288 | bytes 3145728
  27.8 1.7 %copy.74 = f32[32,8,16,128]{3,2,1,0:T(8,128)} copy(f32[32,8,16,128]{3,1,2,0:T(8,128)S(1)} %convert_bitcast_fusion.1) | data formatting | bytes 4194304
  29.6 3.1 %copy.51 = f32[256,2,8,128]{0,2,3,1:T(8,128)} copy(f32[256,2,8,128]{3,2,1,0:T(8,128)} %bitcast.120) | data formatting | bytes 4194304 | tf_op jit(solution)/shard_map/reshape | solution.py:78
  32.8 3.1 %multiply_bitcast_fusion = f32[2,8,256,128]{2,1,3,0:T(8,128)} fusion(f32[256,2,8,128]{0,2,3,1:T(8,128)} %copy.51, f32[2,8]{1,0:T(2,128)S(1)} %mul.232), kind=kLoop, calls=%fused_computation.16 | loop fusion | flops 524288 | bytes 4194368 | tf_op jit(solution)/shard_map/transpose | solution.py:34
  35.9 2.7 %reshape.143 = f32[2,2048,128]{1,2,0:T(8,128)} reshape(f32[2,8,256,128]{2,1,3,0:T(8,128)} %multiply_bitcast_fusion) | data formatting | bytes 4194304 | tf_op jit(solution)/shard_map/reshape | solution.py:35
  38.6 13.6 %all_gather.9 = bf16[192,256]{1,0:T(8,128)(2,1)S(1)} all-gather(bf16[48,256]{1,0:T(8,128)(2,1)S(1)} %copy-done.5), channel_id=1, replica_groups=mesh['parts'=2,'seq'=4,'tensor'=4] {'seq'}, dimensions={0}, use_global_device_ids=true | all-gather | bytes 122880 | tf_op jit(solution)/shard_map/all_gather | solution.py:157
  52.3 0.6 fusion.33
  52.9 0.9 %copy-done.3 = f32[2,2048,128]{1,2,0:T(8,128)S(1)} copy-done((f32[2,2048,128]{1,2,0:T(8,128)S(1)}, f32[2,2048,128]{1,2,0:T(8,128)}, u32[]{:S(2)}) %copy-start.3) | copy-done | bytes 2097176
  55.0 0.6 multiply_convert_fusion
  56.9 0.8 pad_maximum_fusion
  57.7 2.3 %convolution_multiply_fusion = f32[2,2048,128]{2,1,0:T(8,128)S(1)} fusion(bf16[2,2048,192]{1,2,0:T(8,128)(2,1)} %copy-done.1, bf16[192,256]{1,0:T(8,128)(2,1)S(1)} %all_gather.8), kind=kOutput, calls=%fused_computation.2 | convolution fusion | flops 201850880 | bytes 3768320 | tf_op jit(solution)/shard_map/while/body/eval_jaxpr/cmn,ncd->cmd/dot_general | solution.py:127
  60.1 1.3 %copy-done = f32[2,2048,128]{2,1,0:T(8,128)} copy-done((f32[2,2048,128]{2,1,0:T(8,128)}, f32[2,2048,128]{2,1,0:T(8,128)S(1)}, u32[]{:S(2)}) %copy-start) | copy-done | bytes 2097176
  61.4 1.5 %fusion.6 = f32[256,16]{1,0:T(8,128)S(1)} fusion(f32[256,16,128]{2,1,0:T(8,128)S(1)} %bitcast.115, f32[128]{0:T(128)S(1)} %copy-done.6, f32[256,2,8,128]{3,0,2,1:T(8,128)S(1)} %bitcast.116), kind=kLoop, calls=%fused_computation.14 | loop fusion | flops 1568768 | bytes 4211200 | tf_op jit(solution)/shard_map/reduce_sum | solution.py:24
  63.0 2.8 %copy.56 = f32[256,2,8,128]{3,2,1,0:T(8,128)S(1)} copy(f32[256,2,8,128]{3,0,2,1:T(8,128)} %bitcast.117) | data formatting | bytes 4194304 | tf_op jit(solution)/shard_map/transpose | solution.py:44
  67.3 0.6 mul.242
  67.9 3.6 %fusion.3 = bf16[256,2048]{1,0:T(8,128)(2,1)} fusion(bf16[256,2048]{1,0:T(8,128)(2,1)S(1)} %copy-done.2, f32[32,8,16,128]{3,2,1,0:T(8,128)S(1)} %bitcast.122, f32[32,8,16,128]{3,2,1,0:T(8,128)S(1)} %bitcast.124, f32[32,8,16,128]{3,2,1,0:T(8,128)S(1)} %bitcast.121, f32[32,8,16,128]{3,2,1,0:T(8,128)S(1)} %bitcast.123, f32[2048]{0:T(1024)S(1)} %broadcast_bitcast_fusion), kind=kLoop, calls=%fused_computation.9 | loop fusion | flops 3670016 | bytes 10493952 | tf_op jit(solution)/shard_map/convert_element_type | solution.py:165
  71.5 7.8 %reduce-scatter.2.cloned.1.call-done = f32[48,512]{1,0:T(8,128)} async-done(((f32[192,512]{1,0:T(8,128)}), f32[48,512]{1,0:T(8,128)}) %reduce-scatter.2.cloned.1.call-update) | async-done | bytes 98320 | tf_op jit(solution)/shard_map/reduce_scatter | solution.py:160
  79.3 0.8 slice.9
  80.3 1.4 %slice.13 = bf16[48,256]{1,0:T(8,128)(2,1)} slice(f32[48,512]{1,0:T(8,128)} %reduce-scatter.2.cloned.1.call-done), slice={[0:48], [256:512]} | slice | bytes 49152 | tf_op jit(solution)/shard_map/slice | solution.py:173
  81.9 1.4 %fusion.29 = bf16[48,256]{1,0:T(8,128)(2,1)} fusion(f32[6,8,2,128]{3,2,1,0:T(2,128)S(1)} %bitcast.127, f32[6,8,2,128]{3,2,1,0:T(2,128)S(1)} %bitcast.128, f32[6,8,2,128]{3,2,1,0:T(2,128)S(1)} %bitcast.126, f32[256]{0:T(256)S(1)} %broadcast_bitcast_fusion.1, bf16[48,256]{1,0:T(8,128)(2,1)S(1)} %copy-done.4, f32[48,512]{1,0:T(8,128)} %reduce-scatter.2.cloned.1.call-done), kind=kLoop, calls=%fused_computation.43 | loop fusion | flops 86016 | bytes 246784 | tf_op jit(solution)/shard_map/convert_element_type | solution.py:171
  (48 shorter events, 5.6 us)
Async XLA Ops:
  7.2 72.1 %reduce-scatter.2.cloned.1.call-start = ((), (), s32[]{:S(2)}) async-start(), calls=%async_computation.1 | async-start | bytes 491520 | tf_op jit(solution)/shard_map/reduce_scatter | solution.py:160
  9.1 0.9 copy-start.6
  10.0 1.0 %copy-start.4 = (bf16[48,256]{1,0:T(8,128)(2,1)S(1)}, bf16[48,256]{1,0:T(8,128)(2,1)}, u32[]{:S(2)}) copy-start(bf16[48,256]{1,0:T(8,128)(2,1)} %param.8) | copy-start | bytes 73732
  10.0 1.2 %copy-start.7 = (f32[128]{0:T(128)S(1)}, f32[128]{0:T(128)}, u32[]{:S(2)}) copy-start(f32[128]{0:T(128)} %param.11) | copy-start | bytes 1540
  29.6 3.1 %copy-start.8 = (f32[16]{0:T(128)S(1)}, f32[16]{0:T(128)}, u32[]{:S(2)}) copy-start(f32[16]{0:T(128)} %param.12) | copy-start | bytes 196
  35.9 2.8 %copy-start.5 = (bf16[48,256]{1,0:T(8,128)(2,1)S(1)}, bf16[48,256]{1,0:T(8,128)(2,1)}, u32[]{:S(2)}) copy-start(bf16[48,256]{1,0:T(8,128)(2,1)} %param.9) | copy-start | bytes 73732
  52.3 1.6 %copy-start.3 = (f32[2,2048,128]{1,2,0:T(8,128)S(1)}, f32[2,2048,128]{1,2,0:T(8,128)}, u32[]{:S(2)}) copy-start(f32[2,2048,128]{1,2,0:T(8,128)} %reshape.143) | copy-start | bytes 6291460
  55.7 1.2 %copy-start.1 = (bf16[2,2048,192]{1,2,0:T(8,128)(2,1)}, bf16[2,2048,192]{1,2,0:T(8,128)(2,1)S(1)}, u32[]{:S(2)}) copy-start(bf16[2,2048,192]{1,2,0:T(8,128)(2,1)S(1)} %multiply_convert_fusion) | copy-start | bytes 4718596
  60.0 1.4 %copy-start = (f32[2,2048,128]{2,1,0:T(8,128)}, f32[2,2048,128]{2,1,0:T(8,128)S(1)}, u32[]{:S(2)}) copy-start(f32[2,2048,128]{2,1,0:T(8,128)S(1)} %convolution_multiply_fusion) | copy-start | bytes 6291460
  66.7 1.2 %copy-start.2 = (bf16[256,2048]{1,0:T(8,128)(2,1)S(1)}, bf16[256,2048]{1,0:T(8,128)(2,1)}, u32[]{:S(2)}) copy-start(bf16[256,2048]{1,0:T(8,128)(2,1)} %param.7) | copy-start | bytes 3145732
Sparse Core Ops, SparseCore 0:
  57.8 21.4 reduce-scatter.1
where the time goes:
time: 90.8 us; the launch traced here: 90.2 us
  blocking collectives  28.7 us (32%)
  local copies, waits for them, and re-layouts  19.1 us (21%)
  other arithmetic  15 us (17%)
  between operations  14.3 us (16%)
  waiting for transfers between devices  7.82 us (9%)
  matrix products  5.39 us (6%)
    all_gather x1, blocking collectives, shards(): lax.all_gather(k_flat, 'seq', axis=0, tiled=True)  15 us
    all_gather x1, blocking collectives, shards(): lax.all_gather(values, 'seq', axis=0, tiled=True)  13.6 us
    reduce_scatter x1, waiting for transfers between devices, shards(): kv_grads = lax.psum_scatter(buffer, 'seq', scatter_dimension=0, tiled=True)  7.8 us
    unnamed x20, local copies, waits for them, and re-layouts  4.99 us
    transpose x2, other arithmetic, to_groups(): return wide.reshape(count_rows, kv_heads, head_group, head_width).transpo...  3.81 us
    convert_element_type x1, other arithmetic, shards(): query_grad = rms_norm_backward(q_wide, q_recip, q_gain, query_wide).resha...  3.57 us
    reshape x1, local copies, waits for them, and re-layouts, shards(): grad_out.astype(jnp.float32).reshape(text_rows, q_heads, HEAD_SIZE)  3.13 us
    unnamed x2, other arithmetic  2.91 us
  transfers between devices with their start and end apart: 1, of which 1 were waited for; matrix products, arithmetic and copies ran while one was open for 14% of the time, Pallas kernels for 0%

commit v1 on v0

v1 whole, which is shorter than its diff:
```python
import functools
import math

import jax
import jax.numpy as jnp
from jax import lax
from jax.experimental import pallas as pl
from jax.experimental.pallas import tpu as pltpu
from jax.sharding import PartitionSpec as P

HEAD_SIZE = 128
EPS = 1e-05
MESH = pl.DeviceIdType.MESH


def contract(a, b, dims):
    return lax.dot_general(a, b, (dims, ((), ())), preferred_element_type=jnp.float32)


def kernel(n, q_heads, kv_heads, text, rows,
           q_hbm, k_hbm, v_hbm, qg_ref, kg_ref, gate_ref, go_hbm,
           qout_ref, kout_ref, vout_ref,
           q_buf, go_buf, qn_buf, recip_buf, k_raw, kv_buf, gs_buf, acc, send_buf, recv_buf,
           q_sem, go_sem, kv_in_sem, g_send, g_recv, r_send, r_recv):
    me = lax.axis_index("seq")
    peers = [lax.rem(me + d, n) for d in range(1, n)]
    group = q_heads // kv_heads
    scale = 1.0 / math.sqrt(HEAD_SIZE)
    exp2_scale = scale * math.log2(math.e)
    mine = pl.ds(pl.multiple_of(me * rows, 16), rows)

    barrier = pltpu.get_barrier_semaphore()
    for p in peers:
        pl.semaphore_signal(barrier, inc=1, device_id={"seq": p}, device_id_type=MESH)

    def col(h):
        return pl.ds(pl.multiple_of(h * HEAD_SIZE, HEAD_SIZE), HEAD_SIZE)

    def q_copy(h):
        return pltpu.make_async_copy(q_hbm.at[:, col(h)], q_buf.at[h], q_sem.at[h])

    def go_copy(h):
        return pltpu.make_async_copy(go_hbm.at[:, col(h)], go_buf.at[h], go_sem.at[h])

    loads = []
    for c in range(kv_heads):
        loads.append(pltpu.make_async_copy(k_hbm.at[:, col(c)], k_raw.at[c], kv_in_sem.at[c]))
        loads.append(
            pltpu.make_async_copy(
                v_hbm.at[:, col(c)], kv_buf.at[kv_heads + c, mine, :], kv_in_sem.at[kv_heads + c]
            )
        )
    for copy in loads:
        copy.start()

    def start_inputs(h, carry):
        q_copy(h).start()
        go_copy(h).start()
        return carry

    lax.fori_loop(0, q_heads, start_inputs, 0)

    for copy in loads:
        copy.wait()
    for c in range(kv_heads):
        wide = k_raw[c].astype(jnp.float32)
        recip = lax.rsqrt(jnp.mean(wide * wide, axis=-1, keepdims=True) + EPS)
        kv_buf[c, mine, :] = (wide * recip * kg_ref[...]).astype(jnp.bfloat16)

    pl.semaphore_wait(barrier, n - 1)

    def gather_copy(d):
        return pltpu.make_async_remote_copy(
            src_ref=kv_buf.at[:, mine, :],
            dst_ref=kv_buf.at[:, mine, :],
            send_sem=g_send.at[d],
            recv_sem=g_recv.at[me],
            device_id={"seq": peers[d]},
            device_id_type=MESH,
        )

    def gather_landed(d):
        p = peers[d]
        there = pl.ds(pl.multiple_of(p * rows, 16), rows)
        return pltpu.make_async_remote_copy(
            src_ref=kv_buf.at[:, mine, :],
            dst_ref=kv_buf.at[:, there, :],
            send_sem=g_send.at[d],
            recv_sem=g_recv.at[p],
            device_id={"seq": p},
            device_id_type=MESH,
        )

    for d in range(n - 1):
        gather_copy(d).start()

    gates = jnp.tanh(gate_ref[...])
    lane = lax.broadcasted_iota(jnp.int32, gates.shape, 1)

    def prepare(h, carry):
        q_copy(h).wait()
        wide = q_buf[h].astype(jnp.float32)
        recip = lax.rsqrt(jnp.mean(wide * wide, axis=-1, keepdims=True) + EPS)
        recip_buf[h] = recip
        qn_buf[h] = (wide * recip * qg_ref[...]).astype(jnp.bfloat16)
        go_copy(h).wait()
        gate = jnp.sum(jnp.where(lane == h, gates, 0.0), axis=1, keepdims=True)
        go_buf[h] = (go_buf[h].astype(jnp.float32) * gate).astype(jnp.bfloat16)
        return carry

    lax.fori_loop(0, q_heads, prepare, 0)

    for d in range(n - 1):
        gather_landed(d).wait_recv()

    def reduce_copy(c, d):
        return pltpu.make_async_remote_copy(
            src_ref=send_buf.at[c, peers[d]],
            dst_ref=recv_buf.at[c, me],
            send_sem=r_send.at[c, d],
            recv_sem=r_recv.at[c, me],
            device_id={"seq": peers[d]},
            device_id_type=MESH,
        )

    def reduce_landed(c, d):
        return pltpu.make_async_remote_copy(
            src_ref=send_buf.at[c, peers[d]],
            dst_ref=recv_buf.at[c, peers[d]],
            send_sem=r_send.at[c, d],
            recv_sem=r_recv.at[c, peers[d]],
            device_id={"seq": peers[d]},
            device_id_type=MESH,
        )

    for c in range(kv_heads):
        acc[c] = jnp.zeros(acc.shape[1:], jnp.float32)

        def terms(i, carry):
            h = c * group + i
            qn = qn_buf[h]
            go = go_buf[h]
            logits = contract(kv_buf[c], qn, ((1,), (1,)))
            probs = contract(kv_buf[kv_heads + c], go, ((1,), (1,)))
            exps = jnp.exp2(logits * exp2_scale)
            inverse = 1.0 / jnp.sum(exps, axis=0, keepdims=True)
            weights = exps * inverse
            delta = jnp.sum(weights * probs, axis=0, keepdims=True)
            grads = (weights * (probs - delta)).astype(jnp.bfloat16)
            gs_buf[h] = grads
            acc[c, 1] += contract(weights.astype(jnp.bfloat16), go, ((1,), (0,)))
            acc[c, 0] += contract(grads, qn, ((1,), (0,)))
            return carry

        lax.fori_loop(0, group, terms, 0)
        for p in range(n):
            for t in range(2):
                send_buf[c, p, t] = acc[c, t, p * rows:(p + 1) * rows, :].astype(jnp.bfloat16)
        for d in range(n - 1):
            reduce_copy(c, d).start()

    for c in range(kv_heads):

        def query_side(i, carry):
            h = c * group + i
            upstream = contract(gs_buf[h], kv_buf[c], ((0,), (0,))) * scale
            wide = q_buf[h].astype(jnp.float32)
            recip = recip_buf[h]
            scaled = qg_ref[...] * upstream
            mean = jnp.mean(wide * scaled, axis=-1, keepdims=True)
            out = recip * scaled - wide * ((recip * recip * recip) * mean)
            qout_ref[:, col(h)] = out.astype(jnp.bfloat16)
            return carry

        lax.fori_loop(0, group, query_side, 0)

    for c in range(kv_heads):
        key_sum = acc[c, 0, mine, :]
        value_sum = acc[c, 1, mine, :]
        for d in range(n - 1):
            reduce_landed(c, d).wait_recv()
            key_sum += recv_buf[c, peers[d], 0].astype(jnp.float32)
            value_sum += recv_buf[c, peers[d], 1].astype(jnp.float32)
        wide = k_raw[c].astype(jnp.float32)
        recip = lax.rsqrt(jnp.mean(wide * wide, axis=-1, keepdims=True) + EPS)
        scaled = kg_ref[...] * (key_sum * scale)
        mean = jnp.mean(wide * scaled, axis=-1, keepdims=True)
        out = recip * scaled - wide * ((recip * recip * recip) * mean)
        lanes = slice(c * HEAD_SIZE, (c + 1) * HEAD_SIZE)
        kout_ref[:, lanes] = out.astype(jnp.bfloat16)
        vout_ref[:, lanes] = value_sum.astype(jnp.bfloat16)

    for d in range(n - 1):
        gather_copy(d).wait_send()
        for c in range(kv_heads):
            reduce_copy(c, d).wait_send()


def shards(n, query, keys, values, q_gain, key_norm_gain, gate, grad_out):
    text = query.shape[0]
    q_heads = query.shape[1] // HEAD_SIZE
    kv_heads = keys.shape[1] // HEAD_SIZE
    rows = keys.shape[0]
    frames = n * rows
    bf16, f32 = jnp.bfloat16, jnp.float32
    any_spec = pl.BlockSpec(memory_space=pl.ANY)
    vmem = pl.BlockSpec(memory_space=pltpu.VMEM)
    dma = pltpu.SemaphoreType.DMA
    return pl.pallas_call(
        functools.partial(kernel, n, q_heads, kv_heads, text, rows),
        out_shape=(
            jax.ShapeDtypeStruct(query.shape, bf16),
            jax.ShapeDtypeStruct(keys.shape, bf16),
            jax.ShapeDtypeStruct(values.shape, bf16),
        ),
        in_specs=[any_spec, any_spec, any_spec, vmem, vmem, vmem, any_spec],
        out_specs=(vmem, vmem, vmem),
        scratch_shapes=[
            pltpu.VMEM((q_heads, text, HEAD_SIZE), bf16),
            pltpu.VMEM((q_heads, text, HEAD_SIZE), bf16),
            pltpu.VMEM((q_heads, text, HEAD_SIZE), bf16),
            pltpu.VMEM((q_heads, text, 1), f32),
            pltpu.VMEM((kv_heads, rows, HEAD_SIZE), bf16),
            pltpu.VMEM((2 * kv_heads, frames, HEAD_SIZE), bf16),
            pltpu.VMEM((q_heads, frames, text), bf16),
            pltpu.VMEM((kv_heads, 2, frames, HEAD_SIZE), f32),
            pltpu.VMEM((kv_heads, n, 2, rows, HEAD_SIZE), bf16),
            pltpu.VMEM((kv_heads, n, 2, rows, HEAD_SIZE), bf16),
            dma((q_heads,)),
            dma((q_heads,)),
            dma((2 * kv_heads,)),
            dma((n,)),
            dma((n,)),
            dma((kv_heads, n)),
            dma((kv_heads, n)),
        ],
        compiler_params=pltpu.CompilerParams(
            collective_id=0, has_side_effects=True, vmem_limit_bytes=48 * 1024 * 1024
        ),
    )(query, keys, values, q_gain.reshape(1, -1), key_norm_gain.reshape(1, -1), gate.reshape(1, -1), grad_out)


def solution(mesh):
    wide = P(("parts", "seq"), "tensor")
    return jax.shard_map(
        functools.partial(shards, mesh.shape["seq"]),
        mesh=mesh,
        in_specs=(wide, wide, wide, P(), P(), P("tensor"), wide),
        out_specs=(wide, wide, wide),
        check_vma=False,
    )
```

time: 90.8 us -> 31.5 us (0.35)
  blocking collectives: 28.7 us -> 0 us
  Pallas kernels: 0 us -> 23.7 us
  other arithmetic: 15 us -> 0 us
  between operations: 14.3 us -> 0.67 us
  local copies, waits for them, and re-layouts: 19.1 us -> 6.77 us
  waiting for transfers between devices: 7.82 us -> 0 us
  matrix products: 5.39 us -> 0 us
    all_gather x2 -> x0, blocking collectives: 28.7 us -> none  [the longest x1 15 us: shards(): lax.all_gather(k_flat, 'seq', axis=0, tiled=True)]
    pallas_call x0 -> x1, Pallas kernels: none -> 23.7 us  [shards(): pl.pallas_call(functools.partial(kernel, n, q_heads, kv_heads, text, rows...]
    reduce_scatter x1 -> x0, waiting for transfers between devices: 7.8 us -> none  [shards(): kv_grads = lax.psum_scatter(buffer, 'seq', scatter_dimension=0, tiled=True)]
    reshape x5 -> x0, local copies, waits for them, and re-layouts: 5.96 us -> none  [the longest x1 3.13 us: shards(): grad_out.astype(jnp.float32).reshape(text_rows, q_heads, HEAD_SIZE)]
    dot_general x6 -> x0, matrix products: 5.39 us -> none  [the longest x1 2.34 us: backward_terms(): jnp.einsum('cmn,ncd->cmd', grad_scores, key_heads, preferred_element_type...]
    convert_element_type x3 -> x0, other arithmetic: 5.01 us -> none  [the longest x1 3.57 us: shards(): query_grad = rms_norm_backward(q_wide, q_recip, q_gain, query_wide).resha...]
    transpose x2 -> x0, other arithmetic: 3.81 us -> none  [to_groups(): return wide.reshape(count_rows, kv_heads, head_group, head_width).transpo...]
    transpose x2 -> x0, local copies, waits for them, and re-layouts: 3.1 us -> none  [the longest x1 2.82 us: from_groups(): return grouped.reshape(kv_heads, head_group, count_rows, head_width).tran...]
  transfers between devices with their start and end apart: 1 -> 0, of which waited for: 1 -> 0; matrix products, arithmetic and copies ran while one was open for 14% -> 0% of each run, Pallas kernels for 0% -> 0%
where the time goes in v1:
time: 31.5 us; the launch traced here: 31.2 us
  Pallas kernels  23.7 us (75%)
  local copies, waits for them, and re-layouts  6.77 us (21%)
  between operations  0.67 us (2%)
    pallas_call x1, Pallas kernels, shards(): pl.pallas_call(functools.partial(kernel, n, q_heads, kv_heads, text, rows...  23.7 us
    unnamed x17, local copies, waits for them, and re-layouts  6.77 us

profile of v1, /device:TPU:0, one launch (start us, length us, event | category | flops | bytes accessed | tf_op | source)
XLA Modules:
  0.0 31.2 jit_solution(5133089869833658213)
XLA Ops:
  0.6 0.0 copy-start.4
  0.6 0.0 copy-start.5
  0.7 0.0 copy-start.6
  0.7 0.6 %copy-done.4 = f32[128]{0:T(128)S(1)} copy-done((f32[128]{0:T(128)S(1)}, f32[128]{0:T(128)}, u32[]{:S(2)}) %copy-start.4) | copy-done | bytes 536
  1.3 0.0 copy-done.5
  1.3 0.0 copy-done.6
  1.3 0.0 copy-start
  1.3 1.2 %copy-done = bf16[256,2048]{1,0:T(8,128)(2,1)S(1)} copy-done((bf16[256,2048]{1,0:T(8,128)(2,1)S(1)}, bf16[256,2048]{1,0:T(8,128)(2,1)}, u32[]{:S(2)}) %copy-start) | copy-done | bytes 1048600
  2.5 0.0 copy-start.1
  2.5 1.2 %copy-done.1 = bf16[256,2048]{1,0:T(8,128)(2,1)S(1)} copy-done((bf16[256,2048]{1,0:T(8,128)(2,1)S(1)}, bf16[256,2048]{1,0:T(8,128)(2,1)}, u32[]{:S(2)}) %copy-start.1) | copy-done | bytes 1048600
  3.8 0.0 copy-start.2
  3.8 0.7 %copy-done.2 = bf16[48,256]{1,0:T(8,128)(2,1)S(1)} copy-done((bf16[48,256]{1,0:T(8,128)(2,1)S(1)}, bf16[48,256]{1,0:T(8,128)(2,1)}, u32[]{:S(2)}) %copy-start.2) | copy-done | bytes 24600
  4.5 0.0 copy-start.3
  4.5 0.7 %copy-done.3 = bf16[48,256]{1,0:T(8,128)(2,1)S(1)} copy-done((bf16[48,256]{1,0:T(8,128)(2,1)S(1)}, bf16[48,256]{1,0:T(8,128)(2,1)}, u32[]{:S(2)}) %copy-start.3) | copy-done | bytes 24600
  5.2 23.7 %shard_map.94 = (bf16[256,2048]{1,0:T(8,128)(2,1)S(1)}, bf16[48,256]{1,0:T(8,128)(2,1)S(1)}, bf16[48,256]{1,0:T(8,128)(2,1)S(1)}) custom-call(bf16[256,2048]{1,0:T(8,128)(2,1)S(1)} %copy-done, bf16[48,256]{1,0:T(8,128)(2,1)S(1)} %copy-done.2, bf16[48,256]{1,0:T(8,128)(2,1)S(1)} %copy-done.3, f32[1,128]{1,0:T(1,128)S(1)} %bitcast.3, f32[1,128]{1,0:T(1,128)S(1)} %bitcast.4, ...), custom_call_target="tpu_custom_call" | custom-call | tf_op jit(solution)/shard_map/pallas_call | solution.py:209
  29.0 1.0 %copy.13 = bf16[256,2048]{1,0:T(8,128)(2,1)} copy(bf16[256,2048]{1,0:T(8,128)(2,1)S(1)} %get-tuple-element.6) | data formatting | bytes 2097152
  30.0 0.6 %copy.14 = bf16[48,256]{1,0:T(8,128)(2,1)} copy(bf16[48,256]{1,0:T(8,128)(2,1)S(1)} %get-tuple-element.7) | data formatting | bytes 49152
  30.6 0.6 %copy.15 = bf16[48,256]{1,0:T(8,128)(2,1)} copy(bf16[48,256]{1,0:T(8,128)(2,1)S(1)} %get-tuple-element.8) | data formatting | bytes 49152
Async XLA Ops:
  0.6 0.7 %copy-start.4 = (f32[128]{0:T(128)S(1)}, f32[128]{0:T(128)}, u32[]{:S(2)}) copy-start(f32[128]{0:T(128)} %param.10) | copy-start | bytes 1540
  0.6 0.7 %copy-start.5 = (f32[128]{0:T(128)S(1)}, f32[128]{0:T(128)}, u32[]{:S(2)}) copy-start(f32[128]{0:T(128)} %param.11) | copy-start | bytes 1540
  0.7 0.7 %copy-start.6 = (f32[16]{0:T(128)S(1)}, f32[16]{0:T(128)}, u32[]{:S(2)}) copy-start(f32[16]{0:T(128)} %param.12) | copy-start | bytes 196
  1.3 1.2 %copy-start = (bf16[256,2048]{1,0:T(8,128)(2,1)S(1)}, bf16[256,2048]{1,0:T(8,128)(2,1)}, u32[]{:S(2)}) copy-start(bf16[256,2048]{1,0:T(8,128)(2,1)} %q_hbm.1) | copy-start | bytes 3145732
  2.5 1.2 %copy-start.1 = (bf16[256,2048]{1,0:T(8,128)(2,1)S(1)}, bf16[256,2048]{1,0:T(8,128)(2,1)}, u32[]{:S(2)}) copy-start(bf16[256,2048]{1,0:T(8,128)(2,1)} %go_hbm.1) | copy-start | bytes 3145732
  3.8 0.7 %copy-start.2 = (bf16[48,256]{1,0:T(8,128)(2,1)S(1)}, bf16[48,256]{1,0:T(8,128)(2,1)}, u32[]{:S(2)}) copy-start(bf16[48,256]{1,0:T(8,128)(2,1)} %k_hbm.1) | copy-start | bytes 73732
  4.5 0.7 %copy-start.3 = (bf16[48,256]{1,0:T(8,128)(2,1)S(1)}, bf16[48,256]{1,0:T(8,128)(2,1)}, u32[]{:S(2)}) copy-start(bf16[48,256]{1,0:T(8,128)(2,1)} %v_hbm.1) | copy-start | bytes 73732

commit v2 on v1

v2 whole, which is shorter than its diff:
```python
import functools
import math

import jax
import jax.numpy as jnp
from jax import lax
from jax.experimental import pallas as pl
from jax.experimental.pallas import tpu as pltpu
from jax.sharding import PartitionSpec as P

HEAD_SIZE = 128
EPS = 1e-05
MESH = pl.DeviceIdType.MESH
UNROLL = 4
VMEM_LIMIT = 62 * 1024 * 1024


def contract(a, b, dims):
    return lax.dot_general(a, b, (dims, ((), ())), preferred_element_type=jnp.float32)


def kernel(n, q_heads, kv_heads, text, rows,
           q_hbm, k_hbm, v_hbm, qg_hbm, kg_hbm, gate_hbm, go_hbm,
           qout_ref, kout_ref, vout_ref,
           qg_ref, kg_ref, gate_ref, q_buf, go_buf, qn_buf, recip_buf, k_raw, kv_buf, gs_buf, acc, send_buf, recv_buf,
           small_sem, q_sem, go_sem, kv_in_sem, g_send, g_recv, r_send, r_recv):
    me = lax.axis_index("seq")
    peers = [lax.rem(me + d, n) for d in range(1, n)]
    group = q_heads // kv_heads
    scale = 1.0 / math.sqrt(HEAD_SIZE)
    exp2_scale = scale * math.log2(math.e)
    mine = pl.ds(pl.multiple_of(me * rows, 16), rows)

    barrier = pltpu.get_barrier_semaphore()
    for p in peers:
        pl.semaphore_signal(barrier, inc=1, device_id={"seq": p}, device_id_type=MESH)

    def col(h):
        return pl.ds(pl.multiple_of(h * HEAD_SIZE, HEAD_SIZE), HEAD_SIZE)

    def q_copy(h):
        return pltpu.make_async_copy(q_hbm.at[:, col(h)], q_buf.at[h], q_sem.at[h])

    def go_copy(h):
        return pltpu.make_async_copy(go_hbm.at[:, col(h)], go_buf.at[h], go_sem.at[h])

    loads = [
        pltpu.make_async_copy(src, dst, small_sem.at[i])
        for i, (src, dst) in enumerate(
            ((kg_hbm, kg_ref), (qg_hbm, qg_ref), (gate_hbm, gate_ref))
        )
    ]
    for c in range(kv_heads):
        loads.append(pltpu.make_async_copy(k_hbm.at[:, col(c)], k_raw.at[c], kv_in_sem.at[c]))
        loads.append(
            pltpu.make_async_copy(
                v_hbm.at[:, col(c)], kv_buf.at[c, 1, mine, :], kv_in_sem.at[kv_heads + c]
            )
        )
    for copy in loads:
        copy.start()

    def start_inputs(h, carry):
        q_copy(h).start()
        go_copy(h).start()
        return carry

    lax.fori_loop(0, q_heads, start_inputs, 0)

    for copy in loads:
        copy.wait()
    for c in range(kv_heads):
        wide = k_raw[c].astype(jnp.float32)
        recip = lax.rsqrt(jnp.mean(wide * wide, axis=-1, keepdims=True) + EPS)
        kv_buf[c, 0, mine, :] = (wide * recip * kg_ref[...]).astype(jnp.bfloat16)

    pl.semaphore_wait(barrier, n - 1)

    def gather_copy(c, d):
        return pltpu.make_async_remote_copy(
            src_ref=kv_buf.at[c, :, mine, :],
            dst_ref=kv_buf.at[c, :, mine, :],
            send_sem=g_send.at[c, d],
            recv_sem=g_recv.at[c, me],
            device_id={"seq": peers[d]},
            device_id_type=MESH,
        )

    def gather_landed(c, d):
        p = peers[d]
        there = pl.ds(pl.multiple_of(p * rows, 16), rows)
        return pltpu.make_async_remote_copy(
            src_ref=kv_buf.at[c, :, mine, :],
            dst_ref=kv_buf.at[c, :, there, :],
            send_sem=g_send.at[c, d],
            recv_sem=g_recv.at[c, p],
            device_id={"seq": p},
            device_id_type=MESH,
        )

    for c in range(kv_heads):
        for d in range(n - 1):
            gather_copy(c, d).start()

    gates = jnp.tanh(gate_ref[...])
    lane = lax.broadcasted_iota(jnp.int32, gates.shape, 1)

    def prepare(step, carry):
        for u in range(UNROLL):
            h = step * UNROLL + u
            q_copy(h).wait()
            go_copy(h).wait()
        for u in range(UNROLL):
            h = step * UNROLL + u
            wide = q_buf[h].astype(jnp.float32)
            recip = lax.rsqrt(jnp.mean(wide * wide, axis=-1, keepdims=True) + EPS)
            recip_buf[h] = recip
            qn_buf[h] = (wide * recip * qg_ref[...]).astype(jnp.bfloat16)
            gate = jnp.sum(jnp.where(lane == h, gates, 0.0), axis=1, keepdims=True)
            go_buf[h] = (go_buf[h].astype(jnp.float32) * gate).astype(jnp.bfloat16)
        return carry

    lax.fori_loop(0, q_heads // UNROLL, prepare, 0)

    def reduce_copy(c, d):
        return pltpu.make_async_remote_copy(
            src_ref=send_buf.at[c, peers[d]],
            dst_ref=recv_buf.at[c, me],
            send_sem=r_send.at[c, d],
            recv_sem=r_recv.at[c, me],
            device_id={"seq": peers[d]},
            device_id_type=MESH,
        )

    def reduce_landed(c, d):
        return pltpu.make_async_remote_copy(
            src_ref=send_buf.at[c, peers[d]],
            dst_ref=recv_buf.at[c, peers[d]],
            send_sem=r_send.at[c, d],
            recv_sem=r_recv.at[c, peers[d]],
            device_id={"seq": peers[d]},
            device_id_type=MESH,
        )

    for c in range(kv_heads):
        acc[c] = jnp.zeros(acc.shape[1:], jnp.float32)
        for d in range(n - 1):
            gather_landed(c, d).wait_recv()

        def terms(step, carry):
            heads = [c * group + step * UNROLL + u for u in range(UNROLL)]
            qns = [qn_buf[h] for h in heads]
            gos = [go_buf[h] for h in heads]
            logits = [contract(kv_buf[c, 0], qn, ((1,), (1,))) for qn in qns]
            probs = [contract(kv_buf[c, 1], go, ((1,), (1,))) for go in gos]
            value_part, key_part = 0.0, 0.0
            for u, h in enumerate(heads):
                exps = jnp.exp2(logits[u] * exp2_scale)
                inverse = 1.0 / jnp.sum(exps, axis=0, keepdims=True)
                weights = exps * inverse
                delta = jnp.sum(weights * probs[u], axis=0, keepdims=True)
                grads = (weights * (probs[u] - delta)).astype(jnp.bfloat16)
                gs_buf[h] = grads
                value_part += contract(weights.astype(jnp.bfloat16), gos[u], ((1,), (0,)))
                key_part += contract(grads, qns[u], ((1,), (0,)))
            acc[c, 1] += value_part
            acc[c, 0] += key_part
            return carry

        lax.fori_loop(0, group // UNROLL, terms, 0)
        for p in range(n):
            for t in range(2):
                send_buf[c, p, t] = acc[c, t, p * rows:(p + 1) * rows, :].astype(jnp.bfloat16)
        for d in range(n - 1):
            reduce_copy(c, d).start()

    for c in range(kv_heads):

        def query_side(step, carry):
            for u in range(UNROLL):
                h = c * group + step * UNROLL + u
                upstream = contract(gs_buf[h], kv_buf[c, 0], ((0,), (0,))) * scale
                wide = q_buf[h].astype(jnp.float32)
                recip = recip_buf[h]
                scaled = qg_ref[...] * upstream
                mean = jnp.mean(wide * scaled, axis=-1, keepdims=True)
                out = recip * scaled - wide * ((recip * recip * recip) * mean)
                qout_ref[:, col(h)] = out.astype(jnp.bfloat16)
            return carry

        lax.fori_loop(0, group // UNROLL, query_side, 0)

    for c in range(kv_heads):
        key_sum = acc[c, 0, mine, :]
        value_sum = acc[c, 1, mine, :]
        for d in range(n - 1):
            reduce_landed(c, d).wait_recv()
            key_sum += recv_buf[c, peers[d], 0].astype(jnp.float32)
            value_sum += recv_buf[c, peers[d], 1].astype(jnp.float32)
        wide = k_raw[c].astype(jnp.float32)
        recip = lax.rsqrt(jnp.mean(wide * wide, axis=-1, keepdims=True) + EPS)
        scaled = kg_ref[...] * (key_sum * scale)
        mean = jnp.mean(wide * scaled, axis=-1, keepdims=True)
        out = recip * scaled - wide * ((recip * recip * recip) * mean)
        lanes = slice(c * HEAD_SIZE, (c + 1) * HEAD_SIZE)
        kout_ref[:, lanes] = out.astype(jnp.bfloat16)
        vout_ref[:, lanes] = value_sum.astype(jnp.bfloat16)

    for d in range(n - 1):
        for c in range(kv_heads):
            gather_copy(c, d).wait_send()
            reduce_copy(c, d).wait_send()


def shards(n, query, keys, values, q_gain, key_norm_gain, gate, grad_out):
    text = query.shape[0]
    q_heads = query.shape[1] // HEAD_SIZE
    kv_heads = keys.shape[1] // HEAD_SIZE
    rows = keys.shape[0]
    frames = n * rows
    bf16, f32 = jnp.bfloat16, jnp.float32
    any_spec = pl.BlockSpec(memory_space=pl.ANY)
    vmem = pl.BlockSpec(memory_space=pltpu.VMEM)
    dma = pltpu.SemaphoreType.DMA
    return pl.pallas_call(
        functools.partial(kernel, n, q_heads, kv_heads, text, rows),
        out_shape=(
            jax.ShapeDtypeStruct(query.shape, bf16),
            jax.ShapeDtypeStruct(keys.shape, bf16),
            jax.ShapeDtypeStruct(values.shape, bf16),
        ),
        in_specs=[any_spec] * 7,
        out_specs=(vmem, vmem, vmem),
        scratch_shapes=[
            pltpu.VMEM((1, HEAD_SIZE), f32),
            pltpu.VMEM((1, HEAD_SIZE), f32),
            pltpu.VMEM((1, q_heads), f32),
            pltpu.VMEM((q_heads, text, HEAD_SIZE), bf16),
            pltpu.VMEM((q_heads, text, HEAD_SIZE), bf16),
            pltpu.VMEM((q_heads, text, HEAD_SIZE), bf16),
            pltpu.VMEM((q_heads, text, 1), f32),
            pltpu.VMEM((kv_heads, rows, HEAD_SIZE), bf16),
            pltpu.VMEM((kv_heads, 2, frames, HEAD_SIZE), bf16),
            pltpu.VMEM((q_heads, frames, text), bf16),
            pltpu.VMEM((kv_heads, 2, frames, HEAD_SIZE), f32),
            pltpu.VMEM((kv_heads, n, 2, rows, HEAD_SIZE), bf16),
            pltpu.VMEM((kv_heads, n, 2, rows, HEAD_SIZE), bf16),
            dma((3,)),
            dma((q_heads,)),
            dma((q_heads,)),
            dma((2 * kv_heads,)),
            dma((kv_heads, n)),
            dma((kv_heads, n)),
            dma((kv_heads, n)),
            dma((kv_heads, n)),
        ],
        compiler_params=pltpu.CompilerParams(
            collective_id=0, has_side_effects=True, vmem_limit_bytes=VMEM_LIMIT
        ),
    )(query, keys, values, q_gain.reshape(1, -1), key_norm_gain.reshape(1, -1), gate.reshape(1, -1), grad_out)


def solution(mesh):
    wide = P(("parts", "seq"), "tensor")
    return jax.shard_map(
        functools.partial(shards, mesh.shape["seq"]),
        mesh=mesh,
        in_specs=(wide, wide, wide, P(), P(), P("tensor"), wide),
        out_specs=(wide, wide, wide),
        check_vma=False,
    )
```

time: 31.5 us -> 22.6 us (0.72)
  Pallas kernels: 23.7 us -> 18 us
  local copies, waits for them, and re-layouts: 6.77 us -> 3.67 us
    pallas_call x1, Pallas kernels: 23.7 us -> 18 us  [shards(): pl.pallas_call(functools.partial(kernel, n, q_heads, kv_heads, text, rows...]
    unnamed x17 -> x7, local copies, waits for them, and re-layouts: 6.77 us -> 3.67 us
where the time goes in v2:
time: 22.6 us; the launch traced here: 22.3 us
  Pallas kernels  18 us (80%)
  local copies, waits for them, and re-layouts  3.67 us (16%)
  between operations  0.65 us (3%)
    pallas_call x1, Pallas kernels, shards(): pl.pallas_call(functools.partial(kernel, n, q_heads, kv_heads, text, rows...  18 us
    unnamed x7, local copies, waits for them, and re-layouts  3.67 us

profile of v2, /device:TPU:0, one launch (start us, length us, event | category | flops | bytes accessed | tf_op | source)
XLA Modules:
  0.0 22.3 jit_solution(14838007710021943398)
XLA Ops:
  0.6 18.0 %shard_map.94 = (bf16[256,2048]{1,0:T(8,128)(2,1)}, bf16[48,256]{1,0:T(8,128)(2,1)}, bf16[48,256]{1,0:T(8,128)(2,1)}) custom-call(bf16[256,2048]{1,0:T(8,128)(2,1)} %q_hbm.1, bf16[48,256]{1,0:T(8,128)(2,1)} %k_hbm.1, bf16[48,256]{1,0:T(8,128)(2,1)} %v_hbm.1, f32[1,128]{1,0:T(1,128)} %bitcast.3, f32[1,128]{1,0:T(1,128)} %bitcast.4, f32[1,16]{1,0:T(1,128)} %bitcast.5, ...), custom_call_target="tpu_custom_call" | custom-call | tf_op jit(solution)/shard_map/pallas_call | solution.py:225
  18.6 0.0 copy-start.1
  18.6 2.3 %copy.13 = bf16[256,2048]{1,0:T(8,128)(2,1)} copy(bf16[256,2048]{1,0:T(8,128)(2,1)} %get-tuple-element.6) | data formatting | bytes 2097152
  21.0 0.0 copy-done.1
  21.0 0.0 copy-start
  21.0 0.6 %copy.14 = bf16[48,256]{1,0:T(8,128)(2,1)} copy(bf16[48,256]{1,0:T(8,128)(2,1)S(1)} %copy-done.1) | data formatting | bytes 49152
  21.6 0.1 copy-done
  21.7 0.6 %copy.15 = bf16[48,256]{1,0:T(8,128)(2,1)} copy(bf16[48,256]{1,0:T(8,128)(2,1)S(1)} %copy-done) | data formatting | bytes 49152
Async XLA Ops:
  18.6 2.3 %copy-start.1 = (bf16[48,256]{1,0:T(8,128)(2,1)S(1)}, bf16[48,256]{1,0:T(8,128)(2,1)}, u32[]{:S(2)}) copy-start(bf16[48,256]{1,0:T(8,128)(2,1)} %get-tuple-element.7) | copy-start | bytes 73732
  21.0 0.7 %copy-start = (bf16[48,256]{1,0:T(8,128)(2,1)S(1)}, bf16[48,256]{1,0:T(8,128)(2,1)}, u32[]{:S(2)}) copy-start(bf16[48,256]{1,0:T(8,128)(2,1)} %get-tuple-element.8) | copy-start | bytes 73732

commit v3 on v2

--- a/solution.py
+++ b/solution.py
@@ -212,6 +212,15 @@
             reduce_copy(c, d).wait_send()
 
 
+def write_out(q_in, k_in, v_in, q_out, k_out, v_out, sem):
+    pairs = ((q_in, q_out), (k_in, k_out), (v_in, v_out))
+    copies = [pltpu.make_async_copy(a, b, sem.at[i]) for i, (a, b) in enumerate(pairs)]
+    for copy in copies:
+        copy.start()
+    for copy in copies:
+        copy.wait()
+
+
 def shards(n, query, keys, values, q_gain, key_norm_gain, gate, grad_out):
     text = query.shape[0]
     q_heads = query.shape[1] // HEAD_SIZE
@@ -222,12 +231,12 @@
     any_spec = pl.BlockSpec(memory_space=pl.ANY)
     vmem = pl.BlockSpec(memory_space=pltpu.VMEM)
     dma = pltpu.SemaphoreType.DMA
-    return pl.pallas_call(
+    grads = pl.pallas_call(
         functools.partial(kernel, n, q_heads, kv_heads, text, rows),
         out_shape=(
-            jax.ShapeDtypeStruct(query.shape, bf16),
-            jax.ShapeDtypeStruct(keys.shape, bf16),
-            jax.ShapeDtypeStruct(values.shape, bf16),
+            pltpu.VMEM(query.shape, bf16),
+            pltpu.VMEM(keys.shape, bf16),
+            pltpu.VMEM(values.shape, bf16),
         ),
         in_specs=[any_spec] * 7,
         out_specs=(vmem, vmem, vmem),
@@ -258,6 +267,13 @@
             collective_id=0, has_side_effects=True, vmem_limit_bytes=VMEM_LIMIT
         ),
     )(query, keys, values, q_gain.reshape(1, -1), key_norm_gain.reshape(1, -1), gate.reshape(1, -1), grad_out)
+    return pl.pallas_call(
+        write_out,
+        out_shape=tuple(jax.ShapeDtypeStruct(g.shape, g.dtype) for g in grads),
+        in_specs=[vmem] * 3,
+        out_specs=(any_spec,) * 3,
+        scratch_shapes=[dma((3,))],
+    )(*(pltpu.with_memory_space_constraint(g, pltpu.VMEM) for g in grads))
 
 
 def solution(mesh):

time: 22.6 us -> 18.8 us (0.83)
  local copies, waits for them, and re-layouts: 3.67 us -> 0 us
    unnamed x7 -> x0, local copies, waits for them, and re-layouts: 3.67 us -> none
    pallas_call x1, Pallas kernels: 18 us -> 17 us  [shards(): pl.pallas_call(functools.partial(kernel, n, q_heads, kv_heads, text, rows...]
    pallas_call x0 -> x1, Pallas kernels: none -> 1 us  [shards(): pl.pallas_call(write_out, out_shape=tuple((jax.ShapeDtypeStruct(g.shape,...]
where the time goes in v3:
time: 18.8 us; the launch traced here: 18.6 us
  Pallas kernels  18 us (96%)
  between operations  0.64 us (3%)
    pallas_call x1, Pallas kernels, shards(): pl.pallas_call(functools.partial(kernel, n, q_heads, kv_heads, text, rows...  17 us
    pallas_call x1, Pallas kernels, shards(): pl.pallas_call(write_out, out_shape=tuple((jax.ShapeDtypeStruct(g.shape,...  1 us

profile of v3, /device:TPU:0, one launch (start us, length us, event | category | flops | bytes accessed | tf_op | source)
XLA Modules:
  0.0 18.6 jit_solution(2721142367030983984)
XLA Ops:
  0.6 17.0 %shard_map.94 = (bf16[256,2048]{1,0:T(8,128)(2,1)S(1)}, bf16[48,256]{1,0:T(8,128)(2,1)S(1)}, bf16[48,256]{1,0:T(8,128)(2,1)S(1)}) custom-call(bf16[256,2048]{1,0:T(8,128)(2,1)} %q_hbm.1, bf16[48,256]{1,0:T(8,128)(2,1)} %k_hbm.1, bf16[48,256]{1,0:T(8,128)(2,1)} %v_hbm.1, f32[1,128]{1,0:T(1,128)} %bitcast.3, f32[1,128]{1,0:T(1,128)} %bitcast.4, ...), custom_call_target="tpu_custom_call" | custom-call | tf_op jit(solution)/shard_map/pallas_call | solution.py:234
  17.6 1.0 %shard_map.95 = (bf16[256,2048]{1,0:T(8,128)(2,1)}, bf16[48,256]{1,0:T(8,128)(2,1)}, bf16[48,256]{1,0:T(8,128)(2,1)}) custom-call(bf16[256,2048]{1,0:T(8,128)(2,1)S(1)} %get-tuple-element.6.q_in, bf16[48,256]{1,0:T(8,128)(2,1)S(1)} %get-tuple-element.7.k_in, bf16[48,256]{1,0:T(8,128)(2,1)S(1)} %get-tuple-element.8.v_in), custom_call_target="tpu_custom_call" | custom-call | tf_op jit(solution)/shard_map/pallas_call | solution.py:270

commit v4 on v3

--- a/solution.py
+++ b/solution.py
@@ -11,7 +11,7 @@
 HEAD_SIZE = 128
 EPS = 1e-05
 MESH = pl.DeviceIdType.MESH
-UNROLL = 4
+UNROLL = 8
 VMEM_LIMIT = 62 * 1024 * 1024
 
 
@@ -65,8 +65,6 @@
         go_copy(h).start()
         return carry
 
-    lax.fori_loop(0, q_heads, start_inputs, 0)
-
     for copy in loads:
         copy.wait()
     for c in range(kv_heads):
@@ -101,6 +99,8 @@
     for c in range(kv_heads):
         for d in range(n - 1):
             gather_copy(c, d).start()
+
+    lax.fori_loop(0, q_heads, start_inputs, 0)
 
     gates = jnp.tanh(gate_ref[...])
     lane = lax.broadcasted_iota(jnp.int32, gates.shape, 1)

time: 18.8 us -> 18.5 us (0.984)
  Pallas kernels: 18 us -> 17.6 us
    pallas_call x1, Pallas kernels: 17 us -> 16.6 us  [shards(): pl.pallas_call(functools.partial(kernel, n, q_heads, kv_heads, text, rows...]
where the time goes in v4:
time: 18.5 us; the launch traced here: 18.3 us
  Pallas kernels  17.6 us (95%)
  between operations  0.64 us (3%)
    pallas_call x1, Pallas kernels, shards(): pl.pallas_call(functools.partial(kernel, n, q_heads, kv_heads, text, rows...  16.6 us
    pallas_call x1, Pallas kernels, shards(): pl.pallas_call(write_out, out_shape=tuple((jax.ShapeDtypeStruct(g.shape,...  1 us

profile of v4, /device:TPU:0, one launch (start us, length us, event | category | flops | bytes accessed | tf_op | source)
XLA Modules:
  0.0 18.3 jit_solution(3176121441167831683)
XLA Ops:
  0.6 16.6 %shard_map.94 = (bf16[256,2048]{1,0:T(8,128)(2,1)S(1)}, bf16[48,256]{1,0:T(8,128)(2,1)S(1)}, bf16[48,256]{1,0:T(8,128)(2,1)S(1)}) custom-call(bf16[256,2048]{1,0:T(8,128)(2,1)} %q_hbm.1, bf16[48,256]{1,0:T(8,128)(2,1)} %k_hbm.1, bf16[48,256]{1,0:T(8,128)(2,1)} %v_hbm.1, f32[1,128]{1,0:T(1,128)} %bitcast.3, f32[1,128]{1,0:T(1,128)} %bitcast.4, ...), custom_call_target="tpu_custom_call" | custom-call | tf_op jit(solution)/shard_map/pallas_call | solution.py:234
  17.3 1.0 %shard_map.95 = (bf16[256,2048]{1,0:T(8,128)(2,1)}, bf16[48,256]{1,0:T(8,128)(2,1)}, bf16[48,256]{1,0:T(8,128)(2,1)}) custom-call(bf16[256,2048]{1,0:T(8,128)(2,1)S(1)} %get-tuple-element.6.q_in, bf16[48,256]{1,0:T(8,128)(2,1)S(1)} %get-tuple-element.7.k_in, bf16[48,256]{1,0:T(8,128)(2,1)S(1)} %get-tuple-element.8.v_in), custom_call_target="tpu_custom_call" | custom-call | tf_op jit(solution)/shard_map/pallas_call | solution.py:270
